TPU v7x, 256 devices: a whole 4x4x8 slice. The times are simulated.
256 devices in a mesh: dp: 2 (over y_hi), fsdp: 8 (over x, y_lo), expert: 16 (over z, core).
Axes of the slice: x: 4, y: 4 (y_hi: 2, y_lo: 2; y = y_hi * 2 + y_lo), z: 8, core: 2. Of those that a mesh axis runs over, the one named last changes fastest.
Arguments:
- tokens: bfloat16 [65536, 2048], P(('dp', 'fsdp', 'expert')), may hold values from -6 to 6
- expert_ids: int32 [65536, 8], P(('dp', 'fsdp', 'expert')), may hold values from 0 to 127, all different within a row; in each aligned block of 256 rows (0 to 255, 256 to 511, ...) at most 24 rows name the same one
- gate_units: int32 [65536, 8], P(('dp', 'fsdp', 'expert')), may hold values from 1 to 256
- expert_weights: bfloat16 [16, 2048, 3, 768], P('expert', ('dp', 'fsdp')), may hold values from -0.125 to 0.125
- out_grad: bfloat16 [65536, 2048], P(('dp', 'fsdp', 'expert')), may hold values from -6 to 6
Outputs:
- moe_out: bfloat16 [65536, 2048], P(('dp', 'fsdp', 'expert'))
- token_grad: bfloat16 [65536, 2048], P(('dp', 'fsdp', 'expert'))
- weight_grad: bfloat16 [16, 2048, 3, 768], P('expert', ('dp', 'fsdp'))
Inputs may be any that keep to these rules, and one draw needn't show every extreme that they name: `expert_ids`: each row names 8 different experts; the 256 rows of one device name one expert at most 24 times.
All inputs are finite; a program needn't handle non-finite values.
Results may differ from a plain program's by a relative error of at most 0.018.
Values may be sent and summed in bfloat16 or wider, within the bound.
A program may use at most 128 MiB of HBM per device.

v0:
```python
import jax
import jax.numpy as jnp
from jax import lax
from jax.sharding import PartitionSpec as P

CAP = 24


def route_tables(expert_ids, gate_units, expert_count, capacity):
    tok_count, top_count = expert_ids.shape
    slot_count = expert_count * capacity
    flat_ids = expert_ids.reshape(tok_count * top_count)
    chosen = (flat_ids[:, None] == jnp.arange(expert_count, dtype=jnp.int32)[None, :]).astype(
        jnp.int32
    )
    before = jnp.cumsum(chosen, axis=0) - chosen
    ranking = jnp.sum(before * chosen, axis=1)
    inside = flat_ids < expert_count
    slot_of = jnp.where(inside, flat_ids * capacity + ranking, slot_count).reshape(
        tok_count, top_count
    )
    matches = slot_of.T[:, None, :] == jnp.arange(slot_count, dtype=jnp.int32)[None, :, None]
    dispatch = jnp.sum(matches.astype(jnp.int32), axis=0).astype(jnp.bfloat16)
    gate_values = gate_units.astype(jnp.float32) / 256.0
    combine = jnp.sum(jnp.where(matches, gate_values.T[:, None, :], 0.0), axis=0)
    return (dispatch, combine)


def on_device(tokens, expert_ids, gate_units, expert_weights, out_grad):
    expert_count = lax.axis_size("expert")
    dispatch, combine = route_tables(expert_ids, gate_units, expert_count, CAP)
    slot_count = expert_count * CAP
    model_width = tokens.shape[1]
    hidden_units = expert_weights.shape[3]
    send_rows = (
        jnp.dot(dispatch, tokens, preferred_element_type=jnp.float32)
        .astype(jnp.bfloat16)
        .reshape(expert_count, CAP, model_width)
    )
    send_grad = (
        jnp.dot(dispatch, out_grad, preferred_element_type=jnp.float32)
        .astype(jnp.bfloat16)
        .reshape(expert_count, CAP, model_width)
    )
    slot_gate = jnp.sum(combine, axis=1).astype(jnp.bfloat16).reshape(expert_count, CAP)
    recv_rows, recv_grad, recv_gate = (
        lax.all_to_all(send_rows, "expert", split_axis=0, concat_axis=0, tiled=True),
        lax.all_to_all(send_grad, "expert", split_axis=0, concat_axis=0, tiled=True),
        lax.all_to_all(slot_gate, "expert", split_axis=0, concat_axis=0, tiled=True),
    )
    full_weights = lax.all_gather(expert_weights, ("dp", "fsdp"), axis=1, tiled=True)
    flat_weights = full_weights.reshape(model_width, 3 * hidden_units)
    slot_rows = recv_rows.reshape(slot_count, model_width)
    gate_up = jnp.dot(
        slot_rows, flat_weights[:, : 2 * hidden_units], preferred_element_type=jnp.float32
    )
    gate_act = gate_up[:, :hidden_units]
    up_act = gate_up[:, hidden_units:]
    sigmoid_gate = jax.nn.sigmoid(gate_act)
    swish_gate = gate_act * sigmoid_gate
    activation = (swish_gate * up_act).astype(jnp.bfloat16)
    down_rows = flat_weights[:, 2 * hidden_units :]
    result = lax.dot_general(
        activation, down_rows, (((1,), (1,)), ((), ())), preferred_element_type=jnp.float32
    ).astype(jnp.bfloat16)
    returned = lax.all_to_all(
        result.reshape(expert_count, CAP, model_width),
        "expert",
        split_axis=0,
        concat_axis=0,
        tiled=True,
    )
    moe_out = lax.dot_general(
        combine.astype(jnp.bfloat16),
        returned.reshape(slot_count, model_width),
        (((0,), (0,)), ((), ())),
        preferred_element_type=jnp.float32,
    ).astype(jnp.bfloat16)
    grad_rows = recv_grad.reshape(slot_count, model_width)
    scaled = (
        recv_gate.reshape(slot_count, 1).astype(jnp.float32) * grad_rows.astype(jnp.float32)
    ).astype(jnp.bfloat16)
    hidden_grad = jnp.dot(scaled, down_rows, preferred_element_type=jnp.float32)
    gate_grad = (
        hidden_grad * up_act * sigmoid_gate * (1.0 + gate_act * (1.0 - sigmoid_gate))
    ).astype(jnp.bfloat16)
    up_grad = (hidden_grad * swish_gate).astype(jnp.bfloat16)
    pair_grad = jnp.concatenate([gate_grad, up_grad], axis=1)
    row_grad = lax.dot_general(
        pair_grad,
        flat_weights[:, : 2 * hidden_units],
        (((1,), (1,)), ((), ())),
        preferred_element_type=jnp.float32,
    ).astype(jnp.bfloat16)
    back_grads = lax.all_to_all(
        row_grad.reshape(expert_count, CAP, model_width),
        "expert",
        split_axis=0,
        concat_axis=0,
        tiled=True,
    )
    token_grad = lax.dot_general(
        dispatch,
        back_grads.reshape(slot_count, model_width),
        (((0,), (0,)), ((), ())),
        preferred_element_type=jnp.float32,
    ).astype(jnp.bfloat16)
    input_term = lax.dot_general(
        slot_rows, pair_grad, (((0,), (0,)), ((), ())), preferred_element_type=jnp.float32
    )
    down_term = lax.dot_general(
        scaled, activation, (((0,), (0,)), ((), ())), preferred_element_type=jnp.float32
    )
    summed = lax.psum_scatter(
        jnp.concatenate([input_term, down_term], axis=1)
        .reshape(lax.axis_size(("dp", "fsdp")) * expert_weights.shape[1], 3, hidden_units)
        .astype(jnp.bfloat16),
        ("dp", "fsdp"),
        scatter_dimension=0,
        tiled=True,
    )
    weight_grad = summed.reshape(expert_weights.shape)
    return (moe_out, token_grad, weight_grad)


def solution(mesh):
    placed = (
        P(("dp", "fsdp", "expert"), None),
        P(("dp", "fsdp", "expert"), None),
        P(("dp", "fsdp", "expert"), None),
        P("expert", ("dp", "fsdp"), None, None),
        P(("dp", "fsdp", "expert"), None),
    )
    return jax.shard_map(
        on_device,
        mesh=mesh,
        in_specs=placed,
        out_specs=(
            P(("dp", "fsdp", "expert"), None),
            P(("dp", "fsdp", "expert"), None),
            P("expert", ("dp", "fsdp"), None, None),
        ),
        check_vma=False,
    )
```

profile of v0, /device:TPU:5, one launch (start us, length us, event | category | flops | bytes accessed | tf_op | source)
XLA Modules:
  0.0 472.6 jit_solution(17774609145026411051)
XLA Ops:
  7.2 0.0 copy-start
  7.2 0.0 copy-start.3
  7.2 0.0 copy-start.4
  7.2 0.0 all-gather.2.cloned.1.call-start
  7.2 2.2 copy.41
  9.4 0.0 all-gather.2.cloned.1.call-update
  9.5 0.8 copy.38
  10.3 0.1 eq.42
  10.4 0.1 eq.38
  10.5 4.5 reduce-window.6
  15.1 0.4 slice_reduce_fusion
  15.5 0.2 reduce-window.9
  15.7 0.1 broadcast_add_fusion
  15.8 0.1 fusion.15
  15.9 0.1 reduce_sum.39
  16.0 0.1 copy.40
  16.0 0.0 copy-done.4
  16.0 0.0 copy-done.3
  16.1 0.5 select_reduce_fusion
  16.5 0.7 convert_element_type.109
  17.2 9.2 %all-to-all-start.2 = ((bf16[16,1,24]{2,1,0:T(2,128)(2,1)}), bf16[16,1,24]{2,1,0:T(2,128)(2,1)S(1)}, u32[]{:S(2)}, u32[]{:S(2)}) async-start(bf16[16,1,24]{2,1,0:T(2,128)(2,1)} %convert_element_type.109), calls=%async_computation.2 | async-start | bytes 16384 | tf_op jit(solution)/shard_map/all_to_all | solution.py:49
  26.4 0.4 convert_reduce_fusion
  26.8 0.0 copy-done
  26.8 1.8 convolution_convert_fusion.3
  28.5 4.8 %all-to-all-done.2 = bf16[16,1,24]{2,1,0:T(2,128)(2,1)S(1)} async-done(((bf16[16,1,24]{2,1,0:T(2,128)(2,1)}), bf16[16,1,24]{2,1,0:T(2,128)(2,1)S(1)}, u32[]{:S(2)}, u32[]{:S(2)}) %all-to-all-start.2) | async-done | bytes 800 | tf_op jit(solution)/shard_map/all_to_all | solution.py:49
  33.3 4.2 all-to-all-start.3
  37.5 2.9 convolution_convert_fusion.4
  40.4 35.5 %all-to-all-done.3 = bf16[16,24,2048]{2,1,0:T(8,128)(2,1)S(1)} async-done(((bf16[16,24,2048]{2,1,0:T(8,128)(2,1)}), bf16[16,24,2048]{2,1,0:T(8,128)(2,1)S(1)}, u32[]{:S(2)}, u32[]{:S(2)}) %all-to-all-start.3) | async-done | bytes 1572896 | tf_op jit(solution)/shard_map/all_to_all | solution.py:48
  76.0 4.3 all-to-all-start
  80.3 0.2 reduce-scatter.2.cloned.1.call-start
  80.5 0.1 reshape.96
  80.6 1.5 fusion.4
  82.2 36.6 %all-to-all-done = bf16[16,24,2048]{2,1,0:T(8,128)(2,1)} async-done(((bf16[16,24,2048]{2,1,0:T(8,128)(2,1)}), bf16[16,24,2048]{2,1,0:T(8,128)(2,1)}, u32[]{:S(2)}, u32[]{:S(2)}) %all-to-all-start) | async-done | bytes 1572896 | tf_op jit(solution)/shard_map/all_to_all | solution.py:47
  118.8 99.4 %all-gather.2.cloned.1.call-done = bf16[1,2048,3,768]{1,3,2,0:T(8,128)(2,1)} async-done(((bf16[1,128,3,768]{1,3,2,0:T(8,128)(2,1)}), bf16[1,2048,3,768]{1,3,2,0:T(8,128)(2,1)}) %all-gather.2.cloned.1.call-update) | async-done | bytes 9437200 | tf_op jit(solution)/shard_map/all_gather | solution.py:51
  218.2 0.0 copy-start.2
  218.2 5.3 %fusion.2 = f32[384,1536]{1,0:T(8,128)S(1)} fusion(bf16[384,2048]{1,0:T(8,128)(2,1)} %bitcast.4, bf16[2048,2304]{0,1:T(8,128)(2,1)} %bitcast.53), kind=kOutput, calls=%fused_computation.4 | convolution fusion | flops 2415919104 | bytes 10223616 | tf_op jit(solution)/shard_map/dot_general | solution.py:54
  223.5 0.0 copy-done.2
  223.5 3.7 multiply_convert_fusion.1
  227.3 0.0 copy-start.5
  227.3 0.0 copy-start.6
  227.3 1.9 convolution_convert_fusion.1
  229.2 0.0 copy-done.5
  229.2 0.0 copy-done.6
  229.2 5.2 %convolution_convert_fusion = bf16[2048,1536]{0,1:T(8,128)(2,1)S(1)} fusion(bf16[384,2048]{1,0:T(8,128)(2,1)} %bitcast.4, bf16[384,768]{1,0:T(8,128)(2,1)S(1)} %get-tuple-element.6, bf16[384,768]{1,0:T(8,128)(2,1)S(1)} %get-tuple-element.5), kind=kOutput, calls=%fused_computation.1 | convolution fusion | flops 2421424128 | bytes 9043968 | tf_op jit(solution)/shard_map/dot_general | solution.py:108
  234.3 11.5 %pad_maximum_fusion = bf16[2048,2304]{0,1:T(8,128)(2,1)} fusion(bf16[2048,768]{0,1:T(8,128)(2,1)S(1)} %convolution_convert_fusion.1, bf16[2048,1536]{0,1:T(8,128)(2,1)S(1)} %convolution_convert_fusion), kind=kLoop, calls=%fused_computation | loop fusion | flops 18874368 | bytes 18874368 | tf_op jit(solution)/shard_map/concatenate | solution.py:115
  245.9 12.7 %copy.43 = bf16[2048,3,768]{2,0,1:T(8,128)(2,1)} copy(bf16[2048,3,768]{0,2,1:T(8,128)(2,1)} %bitcast.46) | data formatting | bytes 18874368 | tf_op jit(solution)/shard_map/convert_element_type | solution.py:117
  258.6 0.0 reduce-scatter.2.cloned.1.call-update
  258.6 4.5 convolution_convert_fusion.2
  263.0 11.9 %all-to-all-start.1 = ((bf16[16,24,2048]{2,1,0:T(8,128)(2,1)}), bf16[16,24,2048]{2,1,0:T(8,128)(2,1)S(1)}, u32[]{:S(2)}, u32[]{:S(2)}) async-start(bf16[16,24,2048]{2,1,0:T(8,128)(2,1)} %bitcast.50), calls=%async_computation.1 | async-start | bytes 3145728 | tf_op jit(solution)/shard_map/all_to_all | solution.py:66
  274.9 6.9 %fusion.5 = bf16[384,2048]{1,0:T(8,128)(2,1)} fusion(bf16[2048,2304]{0,1:T(8,128)(2,1)} %bitcast.56, bf16[384,768]{1,0:T(8,128)(2,1)} %copy-done.6, bf16[384,768]{1,0:T(8,128)(2,1)} %copy-done.5), kind=kOutput, calls=%fused_computation.14 | convolution fusion | flops 2419064832 | bytes 9043968 | tf_op jit(solution)/shard_map/dot_general | solution.py:89
  281.8 31.5 %all-to-all-done.1 = bf16[16,24,2048]{2,1,0:T(8,128)(2,1)S(1)} async-done(((bf16[16,24,2048]{2,1,0:T(8,128)(2,1)}), bf16[16,24,2048]{2,1,0:T(8,128)(2,1)S(1)}, u32[]{:S(2)}, u32[]{:S(2)}) %all-to-all-start.1) | async-done | bytes 1572896 | tf_op jit(solution)/shard_map/all_to_all | solution.py:66
  313.3 0.0 copy-start.1
  313.3 1.2 copy-done.1
  314.5 4.3 all-to-all-start.4
  318.7 3.1 convolution_convert_fusion.6
  321.9 35.3 %all-to-all-done.4 = bf16[16,24,2048]{2,1,0:T(8,128)(2,1)S(1)} async-done(((bf16[16,24,2048]{2,1,0:T(8,128)(2,1)}), bf16[16,24,2048]{2,1,0:T(8,128)(2,1)S(1)}, u32[]{:S(2)}, u32[]{:S(2)}) %all-to-all-start.4) | async-done | bytes 1572896 | tf_op jit(solution)/shard_map/all_to_all | solution.py:95
  357.2 1.7 convolution_convert_fusion.5
  358.9 106.9 %reduce-scatter.2.cloned.1.call-done = bf16[128,3,768]{2,0,1:T(8,128)(2,1)} async-done(((bf16[2048,3,768]{2,0,1:T(8,128)(2,1)}), bf16[128,3,768]{2,0,1:T(8,128)(2,1)}) %reduce-scatter.2.cloned.1.call-update) | async-done | bytes 589840 | tf_op jit(solution)/shard_map/reduce_scatter | solution.py:114
  (4 shorter events, 0.0 us)
Async XLA Ops:
  7.2 19.6 %copy-start = (bf16[256,2048]{1,0:T(8,128)(2,1)S(1)}, bf16[256,2048]{1,0:T(8,128)(2,1)}, u32[]{:S(2)}) copy-start(bf16[256,2048]{1,0:T(8,128)(2,1)} %param.9) | copy-start | bytes 3145732
  7.2 8.9 %copy-start.3 = (s32[256,8]{0,1:T(8,128)S(1)}, s32[256,8]{0,1:T(8,128)}, u32[]{:S(2)}) copy-start(s32[256,8]{0,1:T(8,128)} %param.6) | copy-start | bytes 24580
  7.2 8.8 %copy-start.4 = (s32[256,8]{0,1:T(8,128)S(1)}, s32[256,8]{0,1:T(8,128)}, u32[]{:S(2)}) copy-start(s32[256,8]{0,1:T(8,128)} %param.7) | copy-start | bytes 24580
  7.2 211.0 %all-gather.2.cloned.1.call-start = ((), (), s32[]{:S(2)}) async-start(), calls=%async_computation.6 | async-start | bytes 10027008 | tf_op jit(solution)/shard_map/all_gather | solution.py:51
  17.2 16.1 %all-to-all-start.2 = ((bf16[16,1,24]{2,1,0:T(2,128)(2,1)}), bf16[16,1,24]{2,1,0:T(2,128)(2,1)S(1)}, u32[]{:S(2)}, u32[]{:S(2)}) async-start(bf16[16,1,24]{2,1,0:T(2,128)(2,1)} %convert_element_type.109), calls=%async_computation.2 | async-start | bytes 16384 | tf_op jit(solution)/shard_map/all_to_all | solution.py:49
  33.3 42.6 %all-to-all-start.3 = ((bf16[16,24,2048]{2,1,0:T(8,128)(2,1)}), bf16[16,24,2048]{2,1,0:T(8,128)(2,1)S(1)}, u32[]{:S(2)}, u32[]{:S(2)}) async-start(bf16[16,24,2048]{2,1,0:T(8,128)(2,1)} %bitcast.8), calls=%async_computation.3 | async-start | bytes 3145728 | tf_op jit(solution)/shard_map/all_to_all | solution.py:48
  76.0 42.8 %all-to-all-start = ((bf16[16,24,2048]{2,1,0:T(8,128)(2,1)}), bf16[16,24,2048]{2,1,0:T(8,128)(2,1)}, u32[]{:S(2)}, u32[]{:S(2)}) async-start(bf16[16,24,2048]{2,1,0:T(8,128)(2,1)} %bitcast.3), calls=%async_computation | async-start | bytes 3145728 | tf_op jit(solution)/shard_map/all_to_all | solution.py:47
  80.3 385.5 %reduce-scatter.2.cloned.1.call-start = ((), (), s32[]{:S(2)}) async-start(), calls=%async_computation.7 | async-start | bytes 10027008 | tf_op jit(solution)/shard_map/reduce_scatter | solution.py:114
  218.2 5.4 %copy-start.2 = (bf16[384,2048]{1,0:T(8,128)(2,1)S(1)}, bf16[384,2048]{1,0:T(8,128)(2,1)}, u32[]{:S(2)}) copy-start(bf16[384,2048]{1,0:T(8,128)(2,1)} %fusion.4) | copy-start | bytes 4718596
  227.3 1.9 copy-start.5
  227.3 1.9 copy-start.6
  263.0 50.3 %all-to-all-start.1 = ((bf16[16,24,2048]{2,1,0:T(8,128)(2,1)}), bf16[16,24,2048]{2,1,0:T(8,128)(2,1)S(1)}, u32[]{:S(2)}, u32[]{:S(2)}) async-start(bf16[16,24,2048]{2,1,0:T(8,128)(2,1)} %bitcast.50), calls=%async_computation.1 | async-start | bytes 3145728 | tf_op jit(solution)/shard_map/all_to_all | solution.py:66
  313.3 1.2 copy-start.1
  314.5 42.7 %all-to-all-start.4 = ((bf16[16,24,2048]{2,1,0:T(8,128)(2,1)}), bf16[16,24,2048]{2,1,0:T(8,128)(2,1)S(1)}, u32[]{:S(2)}, u32[]{:S(2)}) async-start(bf16[16,24,2048]{2,1,0:T(8,128)(2,1)} %bitcast.49), calls=%async_computation.4 | async-start | bytes 3145728 | tf_op jit(solution)/shard_map/all_to_all | solution.py:95
Sparse Core Ops, SparseCore 0:
  10.3 207.7 all-gather.1
  258.7 207.0 reduce-scatter.1
where the time goes:
time: 474 us; the launch traced here: 473 us
  waiting for transfers between devices  350 us (74%)
  matrix products  37 us (8%)
  starting transfers between devices  34 us (7%)
  other arithmetic  18.8 us (4%)
  local copies, waits for them, and re-layouts  18.5 us (4%)
  between operations  14.2 us (3%)
    reduce_scatter x1, waiting for transfers between devices, on_device(): lax.psum_scatter(jnp.concatenate([input_term, down_term], axis=1).reshape...  107 us
    all_gather x1, waiting for transfers between devices, on_device(): lax.all_gather(expert_weights, ('dp', 'fsdp'), axis=1, tiled=True)  99.4 us
    all_to_all x1, waiting for transfers between devices, on_device(): lax.all_to_all(send_rows, 'expert', split_axis=0, concat_axis=0, tiled=True)  36.6 us
    all_to_all x1, waiting for transfers between devices, on_device(): lax.all_to_all(send_grad, 'expert', split_axis=0, concat_axis=0, tiled=True)  35.5 us
    all_to_all x1, waiting for transfers between devices, on_device(): lax.all_to_all(row_grad.reshape(expert_count, CAP, model_width), 'expert'...  35.3 us
    all_to_all x1, waiting for transfers between devices, on_device(): lax.all_to_all(result.reshape(expert_count, CAP, model_width), 'expert',...  31.5 us
    convert_element_type x1, local copies, waits for them, and re-layouts, on_device(): summed = lax.psum_scatter(jnp.concatenate([input_term, down_term], axis=1...  12.7 us
    all_to_all x1, starting transfers between devices, on_device(): lax.all_to_all(result.reshape(expert_count, CAP, model_width), 'expert',...  11.9 us
  transfers between devices with their start and end apart: 7, of which 7 were waited for; matrix products, arithmetic and copies ran while one was open for 6% of the time, Pallas kernels for 0%

commit v1 on v0

--- a/solution.py
+++ b/solution.py
@@ -48,7 +48,12 @@
         lax.all_to_all(send_grad, "expert", split_axis=0, concat_axis=0, tiled=True),
         lax.all_to_all(slot_gate, "expert", split_axis=0, concat_axis=0, tiled=True),
     )
-    full_weights = lax.all_gather(expert_weights, ("dp", "fsdp"), axis=1, tiled=True)
+    full_weights = jnp.concatenate(
+        lax.all_to_all(
+            jnp.stack([expert_weights] * lax.axis_size(("dp", "fsdp"))), ("dp", "fsdp"), 0, 0
+        ),
+        axis=1,
+    )
     flat_weights = full_weights.reshape(model_width, 3 * hidden_units)
     slot_rows = recv_rows.reshape(slot_count, model_width)
     gate_up = jnp.dot(

time: 474 us -> 536 us (1.13)
  waiting for transfers between devices: 350 us -> 381 us
  local copies, waits for them, and re-layouts: 18.5 us -> 49.2 us
    all_to_all x0 -> x1, waiting for transfers between devices: none -> 151 us  [on_device(): lax.all_to_all(jnp.stack([expert_weights] * lax.axis_size(('dp', 'fsdp'))...]
    all_gather x1 -> x0, waiting for transfers between devices: 99.4 us -> none  [on_device(): lax.all_gather(expert_weights, ('dp', 'fsdp'), axis=1, tiled=True)]
    all_to_all x1, waiting for transfers between devices: 36.6 us -> 11.2 us  [on_device(): lax.all_to_all(send_rows, 'expert', split_axis=0, concat_axis=0, tiled=True)]
    all_to_all x0 -> x1, local copies, waits for them, and re-layouts: none -> 13.4 us  [on_device(): lax.all_to_all(jnp.stack([expert_weights] * lax.axis_size(('dp', 'fsdp'))...]
    unnamed x16 -> x18, local copies, waits for them, and re-layouts: 4.21 us -> 14.2 us
    all_to_all x1, starting transfers between devices: 11.9 us -> 4.38 us  [on_device(): lax.all_to_all(result.reshape(expert_count, CAP, model_width), 'expert',...]
    another operation x0 -> x2, local copies, waits for them, and re-layouts: none -> 7.25 us  [the longest x1 5.88 us: on_device(): jnp.stack([expert_weights] * lax.axis_size(('dp', 'fsdp')))]
    all_to_all x0 -> x1, starting transfers between devices: none -> 7.02 us  [on_device(): lax.all_to_all(jnp.stack([expert_weights] * lax.axis_size(('dp', 'fsdp'))...]
  transfers between devices with their start and end apart: 7 -> 7, of which waited for: 7 -> 7; matrix products, arithmetic and copies ran while one was open for 6% -> 9% of each run, Pallas kernels for 0% -> 0%
where the time goes in v1:
time: 536 us; the launch traced here: 535 us
  waiting for transfers between devices  381 us (71%)
  local copies, waits for them, and re-layouts  49.2 us (9%)
  matrix products  36.2 us (7%)
  starting transfers between devices  34 us (6%)
  other arithmetic  20.3 us (4%)
  between operations  14.2 us (3%)
    all_to_all x1, waiting for transfers between devices, on_device(): lax.all_to_all(jnp.stack([expert_weights] * lax.axis_size(('dp', 'fsdp'))...  151 us
    reduce_scatter x1, waiting for transfers between devices, on_device(): lax.psum_scatter(jnp.concatenate([input_term, down_term], axis=1).reshape...  110 us
    all_to_all x1, waiting for transfers between devices, on_device(): lax.all_to_all(send_grad, 'expert', split_axis=0, concat_axis=0, tiled=True)  37.1 us
    all_to_all x1, waiting for transfers between devices, on_device(): lax.all_to_all(row_grad.reshape(expert_count, CAP, model_width), 'expert'...  35.2 us
    all_to_all x1, waiting for transfers between devices, on_device(): lax.all_to_all(result.reshape(expert_count, CAP, model_width), 'expert',...  31.2 us
    unnamed x18, local copies, waits for them, and re-layouts  14.2 us
    all_to_all x1, local copies, waits for them, and re-layouts, on_device(): lax.all_to_all(jnp.stack([expert_weights] * lax.axis_size(('dp', 'fsdp'))...  13.4 us
    convert_element_type x1, local copies, waits for them, and re-layouts, on_device(): summed = lax.psum_scatter(jnp.concatenate([input_term, down_term], axis=1...  12.7 us
  transfers between devices with their start and end apart: 7, of which 7 were waited for; matrix products, arithmetic and copies ran while one was open for 9% of the time, Pallas kernels for 0%

profile of v1, /device:TPU:5, one launch (start us, length us, event | category | flops | bytes accessed | tf_op | source)
XLA Modules:
  0.0 534.6 jit_solution(2456883741183714704)
XLA Ops:
  7.2 0.0 copy-start
  7.2 0.9 copy.41
  8.1 0.1 eq.42
  8.2 0.1 eq.38
  8.3 4.5 reduce-window.6
  12.9 0.4 slice_reduce_fusion
  13.3 0.2 reduce-window.9
  13.5 0.1 broadcast_add_fusion
  13.6 0.1 fusion.15
  13.7 0.1 reduce_sum.39
  13.8 0.1 copy.43
  13.8 0.7 select_bitcast_fusion
  14.6 0.7 multiply_bitcast_fusion
  15.3 0.5 select_reduce_fusion
  15.7 0.7 convert_element_type.109
  16.4 9.2 %all-to-all-start.3 = ((bf16[16,1,24]{2,1,0:T(2,128)(2,1)}), bf16[16,1,24]{2,1,0:T(2,128)(2,1)S(1)}, u32[]{:S(2)}, u32[]{:S(2)}) async-start(bf16[16,1,24]{2,1,0:T(2,128)(2,1)} %convert_element_type.109), calls=%async_computation.3 | async-start | bytes 16384 | tf_op jit(solution)/shard_map/all_to_all | solution.py:49
  25.6 0.4 convert_reduce_fusion
  26.0 0.0 copy-done
  26.0 1.7 convolution_convert_fusion.3
  27.7 4.8 all-to-all-done.3
  32.5 4.2 all-to-all-start.4
  36.7 1.4 copy.44
  38.0 37.1 %all-to-all-done.4 = bf16[16,24,2048]{2,1,0:T(8,128)(2,1)S(1)} async-done(((bf16[16,24,2048]{2,1,0:T(8,128)(2,1)}), bf16[16,24,2048]{2,1,0:T(8,128)(2,1)S(1)}, u32[]{:S(2)}, u32[]{:S(2)}) %all-to-all-start.4) | async-done | bytes 1572896 | tf_op jit(solution)/shard_map/all_to_all | solution.py:48
  75.1 5.9 %stack.2 = bf16[16,1,128,3,768]{2,4,3,1,0:T(8,128)(2,1)} broadcast(bf16[128,3,768]{0,2,1:T(8,128)(2,1)S(1)} %copy.44), dimensions={2,3,4} | broadcast | bytes 10027008 | tf_op jit(solution)/shard_map/stack | solution.py:53
  81.0 0.0 copy-start.4
  81.0 7.0 %all-to-all-start.1 = ((bf16[16,1,128,3,768]{2,4,3,1,0:T(8,128)(2,1)}), bf16[16,1,128,3,768]{2,4,3,1,0:T(8,128)(2,1)}, u32[]{:S(2)}, u32[]{:S(2)}) async-start(bf16[16,1,128,3,768]{2,4,3,1,0:T(8,128)(2,1)} %stack.2), calls=%async_computation.1 | async-start | bytes 18874368 | tf_op jit(solution)/shard_map/all_to_all | solution.py:52
  88.0 0.0 copy-done.4
  88.0 1.8 convolution_convert_fusion.4
  89.8 151.1 %all-to-all-done.1 = bf16[16,1,128,3,768]{2,4,3,1,0:T(8,128)(2,1)} async-done(((bf16[16,1,128,3,768]{2,4,3,1,0:T(8,128)(2,1)}), bf16[16,1,128,3,768]{2,4,3,1,0:T(8,128)(2,1)}, u32[]{:S(2)}, u32[]{:S(2)}) %all-to-all-start.1) | async-done | bytes 9437216 | tf_op jit(solution)/shard_map/all_to_all | solution.py:52
  240.9 4.8 all-to-all-start
  245.7 0.2 reduce-scatter.2.cloned.1.call-start
  246.0 0.1 reshape.95
  246.1 1.6 fusion.4
  247.6 13.4 %copy.45 = bf16[16,1,128,3,768]{2,0,4,3,1:T(8,128)(2,1)} copy(bf16[16,1,128,3,768]{2,4,3,1,0:T(8,128)(2,1)} %all-to-all-done.1) | data formatting | bytes 18874368 | tf_op jit(solution)/shard_map/all_to_all | solution.py:52
  261.0 12.1 %copy.52 = bf16[288,8,16,128]{3,1,2,0:T(8,128)(2,1)} copy(bf16[288,8,16,128]{3,2,1,0:T(8,128)(2,1)} %bitcast.54) | data formatting | bytes 18874368
  273.1 11.2 %all-to-all-done = bf16[16,24,2048]{2,1,0:T(8,128)(2,1)} async-done(((bf16[16,24,2048]{2,1,0:T(8,128)(2,1)}), bf16[16,24,2048]{2,1,0:T(8,128)(2,1)}, u32[]{:S(2)}, u32[]{:S(2)}) %all-to-all-start) | async-done | bytes 1572896 | tf_op jit(solution)/shard_map/all_to_all | solution.py:47
  284.3 0.0 copy-start.3
  284.3 5.4 %fusion.2 = f32[384,1536]{1,0:T(8,128)S(1)} fusion(bf16[384,2048]{1,0:T(8,128)(2,1)} %bitcast.4, bf16[2048,2304]{0,1:T(8,128)(2,1)} %bitcast.55), kind=kOutput, calls=%fused_computation.5 | convolution fusion | flops 2415919104 | bytes 10223616 | tf_op jit(solution)/shard_map/dot_general | solution.py:59
  289.7 0.0 copy-done.3
  289.7 3.7 multiply_convert_fusion.1
  293.4 0.0 copy-start.5
  293.4 0.0 copy-start.7
  293.5 1.9 convolution_convert_fusion.1
  295.3 0.0 copy-done.5
  295.3 0.0 copy-done.7
  295.3 5.2 convolution_convert_fusion
  300.5 11.5 %pad_maximum_fusion = bf16[2048,2304]{0,1:T(8,128)(2,1)} fusion(bf16[2048,768]{0,1:T(8,128)(2,1)S(1)} %convolution_convert_fusion.1, bf16[2048,1536]{0,1:T(8,128)(2,1)S(1)} %convolution_convert_fusion), kind=kLoop, calls=%fused_computation.1 | loop fusion | flops 18874368 | bytes 18874368 | tf_op jit(solution)/shard_map/concatenate | solution.py:120
  312.0 12.7 %copy.47 = bf16[2048,3,768]{2,0,1:T(8,128)(2,1)} copy(bf16[2048,3,768]{0,2,1:T(8,128)(2,1)} %bitcast.53) | data formatting | bytes 18874368 | tf_op jit(solution)/shard_map/convert_element_type | solution.py:122
  324.7 0.0 reduce-scatter.2.cloned.1.call-update
  324.8 4.5 convolution_convert_fusion.2
  329.2 0.0 copy-start.6
  329.2 4.4 all-to-all-start.2
  333.6 0.0 copy-done.6
  333.6 7.2 %fusion.5 = bf16[384,2048]{1,0:T(8,128)(2,1)} fusion(bf16[2048,2304]{0,1:T(8,128)(2,1)} %bitcast.58, bf16[384,768]{1,0:T(8,128)(2,1)} %copy-done.7, bf16[384,768]{1,0:T(8,128)(2,1)S(1)} %copy-done.6), kind=kOutput, calls=%fused_computation.15 | convolution fusion | flops 2419064832 | bytes 9043968 | tf_op jit(solution)/shard_map/dot_general | solution.py:94
  340.8 31.2 %all-to-all-done.2 = bf16[16,24,2048]{2,1,0:T(8,128)(2,1)S(1)} async-done(((bf16[16,24,2048]{2,1,0:T(8,128)(2,1)}), bf16[16,24,2048]{2,1,0:T(8,128)(2,1)S(1)}, u32[]{:S(2)}, u32[]{:S(2)}) %all-to-all-start.2) | async-done | bytes 1572896 | tf_op jit(solution)/shard_map/all_to_all | solution.py:71
  372.0 0.0 copy-start.2
  372.0 1.2 copy-done.2
  373.2 4.3 all-to-all-start.5
  377.4 0.0 copy-start.1
  377.4 3.2 convolution_convert_fusion.6
  380.7 35.2 %all-to-all-done.5 = bf16[16,24,2048]{2,1,0:T(8,128)(2,1)S(1)} async-done(((bf16[16,24,2048]{2,1,0:T(8,128)(2,1)}), bf16[16,24,2048]{2,1,0:T(8,128)(2,1)S(1)}, u32[]{:S(2)}, u32[]{:S(2)}) %all-to-all-start.5) | async-done | bytes 1572896 | tf_op jit(solution)/shard_map/all_to_all | solution.py:100
  415.9 1.7 convolution_convert_fusion.5
  417.6 110.2 %reduce-scatter.2.cloned.1.call-done = bf16[128,3,768]{2,0,1:T(8,128)(2,1)} async-done(((bf16[2048,3,768]{2,0,1:T(8,128)(2,1)}), bf16[128,3,768]{2,0,1:T(8,128)(2,1)}) %reduce-scatter.2.cloned.1.call-update) | async-done | bytes 589840 | tf_op jit(solution)/shard_map/reduce_scatter | solution.py:119
  527.7 0.0 copy-done.1
  (2 shorter events, 0.0 us)
Async XLA Ops:
  7.2 18.8 %copy-start = (bf16[256,2048]{1,0:T(8,128)(2,1)S(1)}, bf16[256,2048]{1,0:T(8,128)(2,1)}, u32[]{:S(2)}) copy-start(bf16[256,2048]{1,0:T(8,128)(2,1)} %param.9) | copy-start | bytes 3145732
  16.4 16.1 %all-to-all-start.3 = ((bf16[16,1,24]{2,1,0:T(2,128)(2,1)}), bf16[16,1,24]{2,1,0:T(2,128)(2,1)S(1)}, u32[]{:S(2)}, u32[]{:S(2)}) async-start(bf16[16,1,24]{2,1,0:T(2,128)(2,1)} %convert_element_type.109), calls=%async_computation.3 | async-start | bytes 16384 | tf_op jit(solution)/shard_map/all_to_all | solution.py:49
  32.5 42.6 %all-to-all-start.4 = ((bf16[16,24,2048]{2,1,0:T(8,128)(2,1)}), bf16[16,24,2048]{2,1,0:T(8,128)(2,1)S(1)}, u32[]{:S(2)}, u32[]{:S(2)}) async-start(bf16[16,24,2048]{2,1,0:T(8,128)(2,1)} %bitcast.8), calls=%async_computation.4 | async-start | bytes 3145728 | tf_op jit(solution)/shard_map/all_to_all | solution.py:48
  81.0 7.0 %copy-start.4 = (bf16[256,2048]{1,0:T(8,128)(2,1)S(1)}, bf16[256,2048]{1,0:T(8,128)(2,1)}, u32[]{:S(2)}) copy-start(bf16[256,2048]{1,0:T(8,128)(2,1)} %param.5) | copy-start | bytes 3145732
  81.0 159.9 %all-to-all-start.1 = ((bf16[16,1,128,3,768]{2,4,3,1,0:T(8,128)(2,1)}), bf16[16,1,128,3,768]{2,4,3,1,0:T(8,128)(2,1)}, u32[]{:S(2)}, u32[]{:S(2)}) async-start(bf16[16,1,128,3,768]{2,4,3,1,0:T(8,128)(2,1)} %stack.2), calls=%async_computation.1 | async-start | bytes 18874368 | tf_op jit(solution)/shard_map/all_to_all | solution.py:52
  240.9 43.4 %all-to-all-start = ((bf16[16,24,2048]{2,1,0:T(8,128)(2,1)}), bf16[16,24,2048]{2,1,0:T(8,128)(2,1)}, u32[]{:S(2)}, u32[]{:S(2)}) async-start(bf16[16,24,2048]{2,1,0:T(8,128)(2,1)} %bitcast.3), calls=%async_computation | async-start | bytes 3145728 | tf_op jit(solution)/shard_map/all_to_all | solution.py:47
  245.7 282.0 %reduce-scatter.2.cloned.1.call-start = ((), (), s32[]{:S(2)}) async-start(), calls=%async_computation.7 | async-start | bytes 10027008 | tf_op jit(solution)/shard_map/reduce_scatter | solution.py:119
  284.3 5.4 %copy-start.3 = (bf16[384,2048]{1,0:T(8,128)(2,1)S(1)}, bf16[384,2048]{1,0:T(8,128)(2,1)}, u32[]{:S(2)}) copy-start(bf16[384,2048]{1,0:T(8,128)(2,1)} %fusion.4) | copy-start | bytes 4718596
  293.4 1.9 copy-start.5
  293.4 1.9 copy-start.7
  329.2 4.4 copy-start.6
  329.2 42.8 %all-to-all-start.2 = ((bf16[16,24,2048]{2,1,0:T(8,128)(2,1)}), bf16[16,24,2048]{2,1,0:T(8,128)(2,1)S(1)}, u32[]{:S(2)}, u32[]{:S(2)}) async-start(bf16[16,24,2048]{2,1,0:T(8,128)(2,1)} %bitcast.62), calls=%async_computation.2 | async-start | bytes 3145728 | tf_op jit(solution)/shard_map/all_to_all | solution.py:71
  372.0 1.2 copy-start.2
  373.2 42.7 %all-to-all-start.5 = ((bf16[16,24,2048]{2,1,0:T(8,128)(2,1)}), bf16[16,24,2048]{2,1,0:T(8,128)(2,1)S(1)}, u32[]{:S(2)}, u32[]{:S(2)}) async-start(bf16[16,24,2048]{2,1,0:T(8,128)(2,1)} %bitcast.61), calls=%async_computation.5 | async-start | bytes 3145728 | tf_op jit(solution)/shard_map/all_to_all | solution.py:100
  377.4 150.3 %copy-start.1 = (bf16[256,2048]{1,0:T(8,128)(2,1)S(1)}, bf16[256,2048]{1,0:T(8,128)(2,1)}, u32[]{:S(2)}) copy-start(bf16[256,2048]{1,0:T(8,128)(2,1)} %param.9) | copy-start | bytes 3145732
Sparse Core Ops, SparseCore 0:
  324.9 202.8 reduce-scatter.1
